TPU v7x, 256 devices: a whole 4x4x8 slice. The times are simulated.
256 devices in a mesh: seq: 64 (over y, z_hi, x), sub: 4 (over z_lo, core).
Axes of the slice: x: 4, y: 4, z: 8 (z_hi: 4, z_lo: 2; z = z_hi * 2 + z_lo), core: 2. Of those that a mesh axis runs over, the one named last changes fastest.
Arguments:
- queries: bfloat16 [65536, 1024], P(('seq', 'sub')), may hold values from -8 to 8
- keys: bfloat16 [65536, 1024], P(('seq', 'sub')), may hold values from -8 to 8
- values: bfloat16 [65536, 1024], P(('seq', 'sub')), may hold values from -8 to 8
Outputs:
- attended: bfloat16 [65536, 1024], P(('seq', 'sub'))
All inputs are finite; a program needn't handle non-finite values.
Results may differ from a plain program's by a relative error of at most 0.0018.
Values may be sent and summed in bfloat16 or wider, within the bound.
A program may use at most 64 MiB of HBM per device.

v0:
```python
import math

import jax
import jax.numpy as jnp
from jax import lax
from jax.experimental import pallas as pl
from jax.experimental.pallas import tpu as pltpu
from jax.sharding import PartitionSpec as P

HEADS = 8
HEAD = 128
LEAF = 128
TOK = 256
FEAT = HEADS * HEAD
UNIT = 2 * HEADS
X, Y, Z, CORES = 4, 4, 8, 2
MESH = pl.DeviceIdType.MESH
F32 = jnp.float32
BF16 = jnp.bfloat16
EXP2_SCALE = math.log2(math.e) / math.sqrt(HEAD)
HIDDEN = -1e30


def averaging_matrix():
    row = lax.broadcasted_iota(jnp.int32, (TOK, TOK), 0)
    tok = lax.broadcasted_iota(jnp.int32, (TOK, TOK), 1)
    result = jnp.zeros((TOK, TOK), F32)
    base = 0
    for level in range(1, 9):
        count = TOK >> level
        first = (row - base) * (1 << level)
        hit = (row >= base) & (row < base + count) & (tok >= first) & (tok < first + (1 << level))
        result = jnp.where(hit, 2.0**-level, result)
        base += count
    return result.astype(BF16)


def kernel(
    q_hbm,
    k_hbm,
    v_hbm,
    out_ref,
    q,
    kv,
    halo,
    own,
    lvl,
    unit,
    zbuf,
    t5,
    t6,
    t7,
    t8,
    spread,
    wide,
    acc,
    top,
    total,
    in_sem,
    send_sem,
    recv_sem,
):
    seq, sub = lax.axis_index("seq"), lax.axis_index("sub")
    x = lax.rem(seq, X)
    zhi = lax.rem(seq // X, Z // 2)
    y = seq // (X * Z // 2)
    c = lax.rem(sub, CORES)
    zlo = sub // CORES
    z = zhi * 2 + zlo
    place = seq * 4 + sub

    def at(xx, yy, zz, cc):
        return {"seq": (yy * (Z // 2) + zz // 2) * X + xx, "sub": lax.rem(zz, 2) * CORES + cc}

    def linear(pos):
        return {"seq": pos // 4, "sub": lax.rem(pos, 4)}

    loads = [
        pltpu.make_async_copy(k_hbm, kv.at[0], in_sem.at[0]),
        pltpu.make_async_copy(v_hbm, kv.at[1], in_sem.at[1]),
        pltpu.make_async_copy(q_hbm, q, in_sem.at[2]),
    ]
    for load in loads:
        load.start()

    x1 = x + 1 - 2 * lax.rem(x, 2)
    y1 = y + 1 - 2 * lax.rem(y, 2)
    z1 = z + 1 - 2 * zlo
    mate = at(x, y, z, 1 - c)
    x_peers = [lax.rem(x + d, X) for d in (1, 2, 3)]
    x_far = [(1 - x // 2) * 2 + j for j in range(2)]
    y_far = [(1 - y // 2) * 2 + j for j in range(2)]
    z_peers = [lax.rem(z + d, Z) for d in range(1, Z)]
    zhi1 = zhi + 1 - 2 * lax.rem(zhi, 2)
    z_near = [zhi1 * 2 + j for j in range(2)]
    z_far = [(1 - zhi // 2) * 4 + j for j in range(4)]
    before = linear(lax.rem(place + 255, 256))
    after = linear(lax.rem(place + 1, 256))
    ends = linear(lax.rem(place + 1 + 254 * (1 - c), 256))

    barrier = pltpu.get_barrier_semaphore()
    greeted = [mate, ends]
    greeted += [at(xx, y, z, c) for xx in x_peers] + [at(xx, y, z1, c) for xx in x_peers]
    greeted += [at(x, yy, z, c) for yy in [y1] + y_far]
    greeted += [at(x, y, zz, c) for zz in z_peers]
    for peer in greeted:
        pl.semaphore_signal(barrier, inc=1, device_id=peer, device_id_type=MESH)

    loads[0].wait()
    loads[1].wait()
    average = averaging_matrix()
    for i in range(2):
        for j in range(4):
            cols = pl.ds(j * 256, 256)
            coarse = jnp.dot(average, kv[i, :, cols], preferred_element_type=F32)
            own[i, :, cols] = coarse.astype(BF16)
            for hh in range(2):
                spread[pl.ds((i * HEADS + j * 2 + hh) * 16, 16), :] = coarse[240:, hh * HEAD : (hh + 1) * HEAD]
    for r in range(16):
        unit[r] = spread[pl.ds(r, UNIT, stride=16), :].astype(BF16)
    zbuf[z] = unit[12:15]

    pl.semaphore_wait(barrier, len(greeted))

    started = []

    def send(src, dst, recv, peer):
        copy = pltpu.make_async_remote_copy(
            src_ref=src,
            dst_ref=dst,
            send_sem=send_sem.at[len(started)],
            recv_sem=recv_sem.at[recv],
            device_id=peer,
            device_id_type=MESH,
        )
        copy.start()
        started.append(copy)

    def arrived(ref, recv):
        pltpu.make_async_copy(ref, ref, recv_sem.at[recv]).wait()

    mine = pl.ds(pl.multiple_of(c * 64, 64), 64)
    for zz in z_peers:
        send(unit.at[pl.ds(12, 3)], zbuf.at[z], 0, at(x, y, zz, c))
    for zz in z_far:
        send(unit.at[pl.ds(8, 4)], t6.at[c, x, lax.rem(z, 4)], 1, at(x, y, zz, c))
    for zz in z_near:
        send(unit.at[pl.ds(0, 8)], t5.at[c, x, zlo], 2, at(x, y, zz, c))
    slot = pl.ds(pl.multiple_of(c * 64 + (lax.rem(x, 2) * 2 + zlo) * 16, 16), 16)
    for xx in x_far:
        for zz in (z, z1):
            send(own.at[:, pl.ds(224, 16)], lvl.at[3, :, slot], 3, at(xx, y, zz, c))
    slot = pl.ds(pl.multiple_of(c * 64 + zlo * 32, 32), 32)
    for zz in (z, z1):
        send(own.at[:, pl.ds(192, 32)], lvl.at[2, :, slot], 4, at(x1, y, zz, c))
    send(own.at[:, pl.ds(128, 64)], lvl.at[1, :, mine], 5, at(x, y, z1, c))
    send(own.at[:, pl.ds(0, 128)], lvl.at[0], 6, mate)
    send(kv.at[:, pl.ds(LEAF, LEAF)], halo.at[0], 7, after)
    send(kv.at[:, pl.ds(0, LEAF)], halo.at[1], 8, before)

    def update(h, scores, values, first=False):
        high = jnp.max(scores, axis=0, keepdims=True)
        if first:
            joint = high
        else:
            old = top[h]
            joint = jnp.maximum(old, high)
            factor = jnp.exp2((old - joint) * EXP2_SCALE)
        weights = jnp.exp2((scores - joint) * EXP2_SCALE)
        weight_sum = jnp.sum(weights, axis=0, keepdims=True)
        fresh = weights.astype(BF16)
        fresh = values(fresh)
        if first:
            total[h] = weight_sum
            acc[h] = fresh
        else:
            total[h] = total[h] * factor + weight_sum
            acc[h] = acc[h] * factor + fresh
        top[h] = joint

    def scored(keys, queries):
        return lax.dot_general(keys, queries, (((1,), (1,)), ((), ())), preferred_element_type=F32)

    def weighted(values, weights):
        return lax.dot_general(values, weights, (((0,), (0,)), ((), ())), preferred_element_type=F32)

    def for_heads(body):
        for h in range(HEADS):
            body(h, pl.ds(h * HEAD, HEAD))

    arrived(zbuf.at[pl.ds(0, 7)], 0)
    send(zbuf.at[:, pl.ds(0, 2)], t7.at[c, x], 9, at(x, y1, z, c))
    for yy in y_far:
        send(zbuf.at[:, 2], t8.at[c, x, lax.rem(y, 2)], 10, at(x, yy, z, c))
    arrived(t6.at[c, x], 1)
    for d in range(3):
        send(t6.at[c, x], t6.at[c, x], 11, at(x_peers[d], y, z, c))
    arrived(t5.at[c, x], 2)
    for d in range(3):
        send(t5.at[c, x], t5.at[c, x], 12, at(x_peers[d], y, z, c))

    loads[2].wait()

    def own_tokens(h, cols):
        scores = scored(kv[0, :, cols], q[:, cols])
        update(h, scores, lambda w: weighted(kv[1, :, cols], w), first=True)

    for_heads(own_tokens)

    arrived(t7.at[c, x], 9)
    for d in range(3):
        send(t7.at[c, x], t7.at[c, x], 13, at(x_peers[d], y, z, c))
    arrived(t8.at[c, x], 10)
    for d in range(3):
        send(t8.at[c, x], t8.at[c, x], 14, at(x_peers[d], y, z, c))

    def level(number):
        def body(h, cols):
            scores = scored(lvl[number, 0, :, cols], q[:, cols])
            update(h, scores, lambda w: weighted(lvl[number, 1, :, cols], w))

        for_heads(body)

    arrived(lvl.at[0], 6)
    level(0)

    for number, recv in ((3, 3), (2, 4), (1, 5)):
        arrived(lvl.at[number, :, mine], recv)
        send(lvl.at[number, :, mine], lvl.at[number, :, mine], 15 + number, mate)

    other = pl.ds(pl.multiple_of((1 - c) * 64, 64), 64)
    for number in (3, 2, 1):
        arrived(lvl.at[number, :, other], 15 + number)
        level(number)

    deep = ((t6, 11, 19), (t5, 12, 20), (t7, 13, 21), (t8, 14, 22))
    for tiles, recv, handed in deep:
        arrived(tiles.at[c, pl.ds(0, 3)], recv)
        send(tiles.at[c], tiles.at[c], handed, mate)

    arrived(halo.at[0], 7)
    arrived(halo.at[1], 8)
    has_before = place > 0
    has_after = place < 255
    lane = lax.broadcasted_iota(jnp.int32, (1, TOK), 1)
    seen = ((lane < LEAF) & has_before) | ((lane >= LEAF) & has_after)

    def halos(h, cols):
        scores = jnp.concatenate(
            [scored(halo[0, 0, :, cols], q[:LEAF, cols]), scored(halo[1, 0, :, cols], q[LEAF:, cols])], axis=1
        )
        scores = jnp.where(seen, scores, HIDDEN)
        update(
            h,
            scores,
            lambda w: jnp.concatenate(
                [weighted(halo[0, 1, :, cols], w[:, :LEAF]), weighted(halo[1, 1, :, cols], w[:, LEAF:])], axis=1
            ),
        )

    for_heads(halos)

    for tiles, _, handed in deep:
        arrived(tiles.at[1 - c], handed)
        wide[...] = tiles[...].astype(F32).reshape(LEAF * UNIT, HEAD)

        def body(h, cols):
            keys = wide[pl.ds(h, LEAF, stride=UNIT), :].astype(BF16)
            scores = scored(keys, q[:, cols])
            update(
                h, scores, lambda w: weighted(wide[pl.ds(HEADS + h, LEAF, stride=UNIT), :].astype(BF16), w)
            )

        for_heads(body)

    def finish(h, cols):
        out_ref[:, cols] = (acc[h] / total[h]).T.astype(BF16)

    for_heads(finish)

    for copy in started:
        copy.wait_send()


def on_device(queries, keys, values):
    return pl.pallas_call(
        kernel,
        out_shape=jax.ShapeDtypeStruct((TOK, FEAT), BF16),
        in_specs=[pl.BlockSpec(memory_space=pl.ANY)] * 3,
        out_specs=pl.BlockSpec(memory_space=pltpu.VMEM),
        scratch_shapes=[
            pltpu.VMEM((TOK, FEAT), BF16),
            pltpu.VMEM((2, TOK, FEAT), BF16),
            pltpu.VMEM((2, 2, LEAF, FEAT), BF16),
            pltpu.VMEM((2, TOK, FEAT), BF16),
            pltpu.VMEM((4, 2, LEAF, FEAT), BF16),
            pltpu.VMEM((16, UNIT, HEAD), BF16),
            pltpu.VMEM((Z, 3, UNIT, HEAD), BF16),
            pltpu.VMEM((CORES, X, 2, 8, UNIT, HEAD), BF16),
            pltpu.VMEM((CORES, X, 4, 4, UNIT, HEAD), BF16),
            pltpu.VMEM((CORES, X, Z, 2, UNIT, HEAD), BF16),
            pltpu.VMEM((CORES, X, 2, Z, UNIT, HEAD), BF16),
            pltpu.VMEM((TOK, HEAD), F32),
            pltpu.VMEM((LEAF * UNIT, HEAD), F32),
            pltpu.VMEM((HEADS, HEAD, TOK), F32),
            pltpu.VMEM((HEADS, 1, TOK), F32),
            pltpu.VMEM((HEADS, 1, TOK), F32),
            pltpu.SemaphoreType.DMA((3,)),
            pltpu.SemaphoreType.DMA((64,)),
            pltpu.SemaphoreType.DMA((23,)),
        ],
        compiler_params=pltpu.CompilerParams(
            collective_id=0, has_side_effects=True, vmem_limit_bytes=48 * 1024 * 1024
        ),
    )(queries, keys, values)


def solution(mesh):
    spec = P(("seq", "sub"), None)
    return jax.shard_map(on_device, mesh=mesh, in_specs=(spec, spec, spec), out_specs=spec, check_vma=False)
```

profile of v0, /device:TPU:1, one launch (start us, length us, event | category | flops | bytes accessed | tf_op | source)
XLA Modules:
  0.0 47.8 jit_solution(18190003074070239999)
XLA Ops:
  0.0 0.0 copy-start
  0.0 1.0 %copy-done = bf16[256,1024]{1,0:T(8,128)(2,1)S(1)} copy-done((bf16[256,1024]{1,0:T(8,128)(2,1)S(1)}, bf16[256,1024]{1,0:T(8,128)(2,1)}, u32[]{:S(2)}) %copy-start) | copy-done | bytes 524312
  1.0 0.0 copy-start.1
  1.0 1.0 %copy-done.1 = bf16[256,1024]{1,0:T(8,128)(2,1)S(1)} copy-done((bf16[256,1024]{1,0:T(8,128)(2,1)S(1)}, bf16[256,1024]{1,0:T(8,128)(2,1)}, u32[]{:S(2)}) %copy-start.1) | copy-done | bytes 524312
  2.1 0.0 copy-start.2
  2.1 1.0 %copy-done.2 = bf16[256,1024]{1,0:T(8,128)(2,1)S(1)} copy-done((bf16[256,1024]{1,0:T(8,128)(2,1)S(1)}, bf16[256,1024]{1,0:T(8,128)(2,1)}, u32[]{:S(2)}) %copy-start.2) | copy-done | bytes 524312
  3.1 43.8 %shard_map.37 = bf16[256,1024]{1,0:T(8,128)(2,1)S(1)} custom-call(bf16[256,1024]{1,0:T(8,128)(2,1)S(1)} %copy-done, bf16[256,1024]{1,0:T(8,128)(2,1)S(1)} %copy-done.1, bf16[256,1024]{1,0:T(8,128)(2,1)S(1)} %copy-done.2), custom_call_target="tpu_custom_call" | custom-call | tf_op jit(solution)/shard_map/pallas_call | solution.py:286
  47.0 0.8 %copy.5 = bf16[256,1024]{1,0:T(8,128)(2,1)} copy(bf16[256,1024]{1,0:T(8,128)(2,1)S(1)} %shard_map.37) | data formatting | bytes 1048576
Async XLA Ops:
  0.0 1.0 %copy-start = (bf16[256,1024]{1,0:T(8,128)(2,1)S(1)}, bf16[256,1024]{1,0:T(8,128)(2,1)}, u32[]{:S(2)}) copy-start(bf16[256,1024]{1,0:T(8,128)(2,1)} %q_hbm.1) | copy-start | bytes 1572868
  1.0 1.0 %copy-start.1 = (bf16[256,1024]{1,0:T(8,128)(2,1)S(1)}, bf16[256,1024]{1,0:T(8,128)(2,1)}, u32[]{:S(2)}) copy-start(bf16[256,1024]{1,0:T(8,128)(2,1)} %k_hbm.1) | copy-start | bytes 1572868
  2.1 1.0 %copy-start.2 = (bf16[256,1024]{1,0:T(8,128)(2,1)S(1)}, bf16[256,1024]{1,0:T(8,128)(2,1)}, u32[]{:S(2)}) copy-start(bf16[256,1024]{1,0:T(8,128)(2,1)} %v_hbm.1) | copy-start | bytes 1572868
where the time goes:
time: 48 us; the launch traced here: 47.8 us
  Pallas kernels  43.8 us (91%)
  local copies, waits for them, and re-layouts  3.92 us (8%)
    pallas_call x1, Pallas kernels, on_device(): pl.pallas_call(kernel, out_shape=jax.ShapeDtypeStruct((TOK, FEAT), BF16),...  43.8 us
    unnamed x7, local copies, waits for them, and re-layouts  3.92 us

commit v1 on v0

v1 whole, which is shorter than its diff:
```python
import math

import jax
import jax.numpy as jnp
from jax import lax
from jax.experimental import pallas as pl
from jax.experimental.pallas import tpu as pltpu
from jax.sharding import PartitionSpec as P

HEADS = 8
HEAD = 128
LEAF = 128
TOK = 256
FEAT = HEADS * HEAD
UNIT = 2 * HEADS
X, Y, Z, CORES = 4, 4, 8, 2
MESH = pl.DeviceIdType.MESH
F32 = jnp.float32
BF16 = jnp.bfloat16
EXP2_SCALE = math.log2(math.e) / math.sqrt(HEAD)
HIDDEN = -1e30


def averaging_matrix():
    row = lax.broadcasted_iota(jnp.int32, (TOK, TOK), 0)
    tok = lax.broadcasted_iota(jnp.int32, (TOK, TOK), 1)
    result = jnp.zeros((TOK, TOK), F32)
    base = 0
    for level in range(1, 9):
        count = TOK >> level
        first = (row - base) * (1 << level)
        hit = (row >= base) & (row < base + count) & (tok >= first) & (tok < first + (1 << level))
        result = jnp.where(hit, 2.0**-level, result)
        base += count
    return result.astype(BF16)


def kernel(
    q_hbm,
    k_hbm,
    v_hbm,
    out_ref,
    q,
    kv,
    halo,
    transit,
    own,
    lvl,
    derived,
    unit,
    ybuf,
    zbuf,
    t5,
    t6,
    t7,
    t8,
    spread,
    wide,
    acc,
    top,
    total,
    in_sem,
    send_sem,
    recv_sem,
    near_sem,
    far_sem,
):
    seq, sub = lax.axis_index("seq"), lax.axis_index("sub")
    x = lax.rem(seq, X)
    zhi = lax.rem(seq // X, Z // 2)
    y = seq // (X * Z // 2)
    c = lax.rem(sub, CORES)
    zlo = sub // CORES
    z = zhi * 2 + zlo
    place = seq * 4 + sub

    def at(xx, yy, zz, cc):
        return {"seq": (yy * (Z // 2) + zz // 2) * X + xx, "sub": lax.rem(zz, 2) * CORES + cc}

    loads = [
        pltpu.make_async_copy(k_hbm, kv.at[0], in_sem.at[0]),
        pltpu.make_async_copy(v_hbm, kv.at[1], in_sem.at[1]),
        pltpu.make_async_copy(q_hbm, q, in_sem.at[2]),
    ]
    for load in loads:
        load.start()

    x1 = x + 1 - 2 * lax.rem(x, 2)
    x3 = X - 1 - x
    y1 = y + 1 - 2 * lax.rem(y, 2)
    y2 = lax.rem(y + 2, Y)
    yp = lax.rem(y, 2)
    z1 = z + 1 - 2 * zlo
    mate = at(x, y, z, 1 - c)
    zhi1 = zhi + 1 - 2 * lax.rem(zhi, 2)
    end_place = lax.rem(place + 1 + 254 * (1 - c), 256)
    end = {"seq": end_place // 4, "sub": lax.rem(end_place, 4)}
    end_zhi = lax.rem(end_place // 16, Z // 2)
    end_near = end_zhi == zhi

    cross = at(x, y, z1, 1 - c)
    near = [(mate, c == 0), (at(x, y, z1, c), zlo == 0), (cross, zlo == 0), (at(x, y1, z, c), y1 > y), (at(x, y2, z, c), y2 > y)]
    near += [(at(xx, y, z, c), xx > x) for xx in [lax.rem(x + d, X) for d in (1, 2, 3)]]
    far_peers = [
        (at(x, y, zz * 2 + j, c), zz > zhi) for zz in [lax.rem(zhi + d, Z // 2) for d in (3, 2, 1)] for j in range(2)
    ]
    others = [peer for peer, _ in far_peers]
    end_far = jnp.logical_not(end_near)
    far_peers += [(end, end_zhi > zhi)]

    barrier = pltpu.get_barrier_semaphore()

    def tell(sem, peer, when):
        @pl.when(when)
        def _():
            pl.semaphore_signal(sem, inc=1, device_id=peer, device_id_type=MESH)

    def count(flags):
        return sum(flag.astype(jnp.int32) for flag in flags)

    def await_count(sem, amount):
        @pl.when(amount > 0)
        def _():
            pl.semaphore_wait(sem, amount)

    for peer, later in far_peers + near:
        tell(barrier, peer, later)
    await_count(
        barrier,
        count([jnp.logical_not(later) for _, later in near + far_peers[:-1]]) + (end_zhi < zhi).astype(jnp.int32),
    )
    for peer, later in far_peers[:-1]:
        tell(far_sem, peer, jnp.logical_not(later))
    tell(far_sem, end, end_zhi < zhi)
    for peer, later in near:
        tell(near_sem, peer, jnp.logical_not(later))

    loads[0].wait()
    loads[1].wait()
    average = averaging_matrix()
    for i in range(2):
        for j in range(4):
            cols = pl.ds(j * 256, 256)
            coarse = jnp.dot(average, kv[i, :, cols], preferred_element_type=F32)
            own[i, :, cols] = coarse.astype(BF16)
            for hh in range(2):
                spread[pl.ds((i * HEADS + j * 2 + hh) * 16, 16), :] = coarse[240:, hh * HEAD : (hh + 1) * HEAD]
    for r in range(16):
        unit[r] = spread[pl.ds(r, UNIT, stride=16), :].astype(BF16)

    await_count(near_sem, count([later for _, later in near]))

    started = []

    def copy_to(src, dst, recv, peer, slot):
        return pltpu.make_async_remote_copy(
            src_ref=src,
            dst_ref=dst,
            send_sem=send_sem.at[slot],
            recv_sem=recv_sem.at[recv],
            device_id=peer,
            device_id_type=MESH,
        )

    def send(src, dst, recv, peer):
        copy = copy_to(src, dst, recv, peer, 14 + len(started))
        copy.start()
        started.append(copy)

    def arrived(ref, recv):
        pltpu.make_async_copy(ref, ref, recv_sem.at[recv]).wait()

    def rows(start, count):
        return pl.ds(pl.multiple_of(start, 16), count)

    mine, other = rows(c * 64, 64), rows((1 - c) * 64, 64)
    outer = c == zlo
    edge = kv.at[:, rows(c * LEAF, LEAF)]
    end_copy = copy_to(edge, halo.at[1 - c], 7, end, 0)
    inner_copy = copy_to(edge, halo.at[1 - c], 7, cross, 0)
    step_copy = copy_to(edge, transit, 43, at(lax.rem(x + 3 + 2 * c, X), y, z, c), 0)
    pass_copy = copy_to(transit, halo.at[1 - c], 7, cross, 100)
    steps = outer & end_near
    passes = outer & (x != 3 * (1 - c))
    far = [copy_to(unit.at[pl.ds(8, 4)], t6.at[c, x, lax.rem(z, 4)], 9, at(x, y, (1 - zhi // 2) * 4 + j, c), 1 + j) for j in range(4)]
    far += [copy_to(unit.at[pl.ds(0, 8)], t5.at[c, x, zlo], 8, at(x, y, zhi1 * 2 + j, c), 5 + j) for j in range(2)]
    gather = [copy_to(ybuf, zbuf.at[z], 10, peer, 7 + j) for j, peer in enumerate(others + [at(x, y, z1, c)])]

    def update(h, lanes, scores, values, first=False):
        high = jnp.max(scores, axis=0, keepdims=True)
        if first:
            joint = high
        else:
            old = top[h, :, lanes]
            joint = jnp.maximum(old, high)
            factor = jnp.exp2((old - joint) * EXP2_SCALE)
        weights = jnp.exp2((scores - joint) * EXP2_SCALE)
        weight_sum = jnp.sum(weights, axis=0, keepdims=True)
        fresh = lax.dot_general(
            values, weights.astype(BF16), (((0,), (0,)), ((), ())), preferred_element_type=F32
        )
        if first:
            total[h, :, lanes] = weight_sum
            acc[h, :, lanes] = fresh
        else:
            total[h, :, lanes] = total[h, :, lanes] * factor + weight_sum
            acc[h, :, lanes] = acc[h, :, lanes] * factor + fresh
        top[h, :, lanes] = joint

    def scored(keys, queries):
        return lax.dot_general(keys, queries, (((1,), (1,)), ((), ())), preferred_element_type=F32)

    def for_heads(body):
        for h in range(HEADS):
            body(h, pl.ds(h * HEAD, HEAD))

    everyone = pl.ds(0, TOK)

    def own_tokens(h, cols):
        update(h, everyone, scored(kv[0, :, cols], q[:, cols]), kv[1, :, cols], first=True)

    def level(number):
        def body(h, cols):
            update(h, everyone, scored(lvl[number, 0, :, cols], q[:, cols]), lvl[number, 1, :, cols])

        for_heads(body)

    def side(which, block):
        lanes = pl.ds(pl.multiple_of(block * LEAF, LEAF), LEAF)

        def body(h, cols):
            update(h, lanes, scored(halo[which, 0, :, cols], q[lanes, cols]), halo[which, 1, :, cols])

        for_heads(body)

    def deep(tiles):
        wide[...] = tiles[...].astype(F32).reshape(LEAF * UNIT, HEAD)

        def body(h, cols):
            keys = wide[pl.ds(h, LEAF, stride=UNIT), :].astype(BF16)
            values = wide[pl.ds(HEADS + h, LEAF, stride=UNIT), :].astype(BF16)
            update(h, everyone, scored(keys, q[:, cols]), values)

        for_heads(body)

    xl, xr, xo = lax.rem(x + 3, X), lax.rem(x + 1, X), lax.rem(x + 2, X)
    xp, xm = at(xr, y, z, c), at(xl, y, z, c)
    p5, p6, p7, p8 = (lambda i: t5.at[c, i]), (lambda i: t6.at[c, i]), (lambda i: t7.at[c, i]), (lambda i: t8.at[c, yp, i])
    h5 = lambda i, j: t5.at[c, i, j]
    h6 = lambda i, j: t6.at[c, i, pl.ds(2 * j, 2)]
    h7 = lambda i, j: t7.at[c, i, pl.ds(4 * j, 4)]

    def spread_x(part, first):
        send(part(x), part(x), first, xp)
        send(part(x), part(x), first + 1, xm)

    def relay_x(part, half, first):
        arrived(part(xl), first)
        send(half(xl, 0), half(xl, 0), first + 2, xp)
        arrived(part(xr), first + 1)
        send(half(xr, 1), half(xr, 1), first + 3, xm)

    def whole_x(half, first):
        arrived(half(xo, 0), first + 2)
        arrived(half(xo, 1), first + 3)

    def far_sends():
        await_count(far_sem, count([later for _, later in far_peers]))
        for copy in far:
            copy.start()
        arrived(ybuf.at[pl.ds(0, 2)], 0)
        arrived(ybuf.at[pl.ds(2, 1)], 1)
        for copy in gather:
            copy.start()


    send(unit.at[pl.ds(12, 2)], ybuf.at[pl.ds(0, 2)], 0, at(x, y1, z, c))
    send(unit.at[pl.ds(14, 1)], ybuf.at[pl.ds(2, 1)], 1, at(x, y2, z, c))
    send(own.at[:, pl.ds(128, 64)], lvl.at[1, :, mine], 6, at(x, y, z1, c))
    send(own.at[:, pl.ds(224, 16)], lvl.at[3, :, rows(c * 64, 16)], 2, at(x3, y, z, c))
    send(own.at[:, pl.ds(192, 32)], lvl.at[2, :, rows(c * 64, 32)], 3, at(x1, y, z, c))

    @pl.when(steps)
    def _():
        step_copy.start()


    @pl.when(end_zhi < zhi)
    def _():
        end_copy.start()

    send(own.at[:, pl.ds(0, 128)], lvl.at[0], 4, mate)
    send(kv.at[:, rows((1 - c) * LEAF, LEAF)], halo.at[c], 5, mate)

    @pl.when(zhi >= 2)
    def _():
        far_sends()

    loads[2].wait()
    for_heads(own_tokens)
    arrived(lvl.at[1, :, mine], 6)
    send(lvl.at[1, :, mine], lvl.at[1, :, mine], 15, mate)
    passed = jnp.concatenate([average[:32, :64], average[128:144, :64]])
    for i in range(2):
        derived[i] = jnp.dot(passed, lvl[1, i, mine], preferred_element_type=F32).astype(BF16)
    send(derived.at[:, pl.ds(32, 16)], lvl.at[3, :, rows(c * 64 + 16, 16)], 26, at(x3, y, z, c))
    send(derived.at[:, pl.ds(0, 32)], lvl.at[2, :, rows(c * 64 + 32, 32)], 12, at(x1, y, z, c))
    arrived(lvl.at[0], 4)
    level(0)
    arrived(halo.at[1 - c], 5)
    side(1 - c, 1 - c)

    @pl.when(zhi < 2)
    def _():
        far_sends()


    @pl.when(end_zhi > zhi)
    def _():
        end_copy.start()

    zbuf[z] = ybuf[...]
    arrived(lvl.at[3, :, rows(c * 64, 16)], 2)
    arrived(lvl.at[3, :, rows(c * 64 + 16, 16)], 26)
    send(lvl.at[3, :, rows(c * 64, 32)], lvl.at[3, :, rows(c * 64 + 32, 32)], 11, at(x1, y, z, c))
    arrived(zbuf.at[pl.ds(0, 7)], 10)
    t8[c, yp, x] = zbuf[:, 2]
    t7[c, x] = zbuf[:, 0:2]
    for d in (1, 2, 3):
        send(p8(x), p8(x), 34 + d, at(lax.rem(x + d, X), y, z, c))
    spread_x(p7, 39)
    arrived(t5.at[c, x], 8)
    spread_x(p5, 27)
    arrived(t6.at[c, x], 9)
    spread_x(p6, 31)

    @pl.when(passes)
    def _():
        arrived(transit, 43)
        pass_copy.start()


    @pl.when(jnp.logical_not(outer))
    def _():
        inner_copy.start()

    arrived(lvl.at[2, :, rows(c * 64, 32)], 3)
    arrived(lvl.at[2, :, rows(c * 64 + 32, 32)], 12)
    send(lvl.at[2, :, mine], lvl.at[2, :, mine], 14, mate)
    arrived(lvl.at[3, :, rows(c * 64 + 32, 32)], 11)
    send(lvl.at[3, :, mine], lvl.at[3, :, mine], 13, mate)
    arrived(lvl.at[2, :, other], 14)
    level(2)
    arrived(lvl.at[1, :, other], 15)
    level(1)
    for d in (1, 2, 3):
        arrived(p8(lax.rem(x + X - d, X)), 34 + d)
    send(t8.at[c, yp], t8.at[c, yp], 20, at(x, y1, z, c))
    send(t8.at[c, yp], t8.at[c, yp], 21, mate)
    relay_x(p7, h7, 39)
    relay_x(p5, h5, 27)
    relay_x(p6, h6, 31)
    arrived(lvl.at[3, :, other], 13)
    level(3)
    arrived(t8.at[c, 1 - yp], 20)
    send(t8.at[c, 1 - yp], t8.at[c, 1 - yp], 25, mate)
    whole_x(h7, 39)
    send(t7.at[c], t7.at[c], 22, mate)
    whole_x(h5, 27)
    send(t5.at[c], t5.at[c], 24, mate)
    whole_x(h6, 31)
    send(t6.at[c], t6.at[c], 23, mate)
    arrived(t8.at[1 - c, yp], 21)
    arrived(t8.at[1 - c, 1 - yp], 25)
    deep(t8)
    arrived(t7.at[1 - c], 22)
    deep(t7)
    arrived(t5.at[1 - c], 24)
    deep(t5)
    arrived(t6.at[1 - c], 23)
    deep(t6)
    arrived(halo.at[c], 7)

    @pl.when((place + c > 0) & (place + c < 256))
    def _():
        side(c, c)


    def finish(h, cols):
        out_ref[:, cols] = (acc[h] / total[h]).T.astype(BF16)

    for_heads(finish)

    @pl.when(passes)
    def _():
        pass_copy.wait_send()

    for copy in [inner_copy] + far + gather + started:
        copy.wait_send()


def on_device(queries, keys, values):
    return pl.pallas_call(
        kernel,
        out_shape=jax.ShapeDtypeStruct((TOK, FEAT), BF16),
        in_specs=[pl.BlockSpec(memory_space=pl.ANY)] * 3,
        out_specs=pl.BlockSpec(memory_space=pltpu.VMEM),
        scratch_shapes=[
            pltpu.VMEM((TOK, FEAT), BF16),
            pltpu.VMEM((2, TOK, FEAT), BF16),
            pltpu.VMEM((2, 2, LEAF, FEAT), BF16),
            pltpu.VMEM((2, LEAF, FEAT), BF16),
            pltpu.VMEM((2, TOK, FEAT), BF16),
            pltpu.VMEM((4, 2, LEAF, FEAT), BF16),
            pltpu.VMEM((2, 48, FEAT), BF16),
            pltpu.VMEM((16, UNIT, HEAD), BF16),
            pltpu.VMEM((3, UNIT, HEAD), BF16),
            pltpu.VMEM((Z, 3, UNIT, HEAD), BF16),
            pltpu.VMEM((CORES, X, 2, 8, UNIT, HEAD), BF16),
            pltpu.VMEM((CORES, X, 4, 4, UNIT, HEAD), BF16),
            pltpu.VMEM((CORES, X, Z, 2, UNIT, HEAD), BF16),
            pltpu.VMEM((CORES, 2, X, Z, UNIT, HEAD), BF16),
            pltpu.VMEM((TOK, HEAD), F32),
            pltpu.VMEM((LEAF * UNIT, HEAD), F32),
            pltpu.VMEM((HEADS, HEAD, TOK), F32),
            pltpu.VMEM((HEADS, 1, TOK), F32),
            pltpu.VMEM((HEADS, 1, TOK), F32),
            pltpu.SemaphoreType.DMA((3,)),
            pltpu.SemaphoreType.DMA((101,)),
            pltpu.SemaphoreType.DMA((44,)),
            pltpu.SemaphoreType.REGULAR,
            pltpu.SemaphoreType.REGULAR,
        ],
        compiler_params=pltpu.CompilerParams(
            collective_id=0, has_side_effects=True, vmem_limit_bytes=24 * 1024 * 1024
        ),
    )(*[pltpu.with_memory_space_constraint(a, pltpu.HBM) for a in (queries, keys, values)])


def solution(mesh):
    spec = P(("seq", "sub"), None)
    return jax.shard_map(on_device, mesh=mesh, in_specs=(spec, spec, spec), out_specs=spec, check_vma=False)
```

time: 48 us -> 43.1 us (0.90)
  the two profiles are of different devices: /device:TPU:1 before, /device:TPU:192 now
where the time goes in v1:
time: 43.1 us; the launch traced here: 43 us
  Pallas kernels  42.2 us (98%)
  local copies, waits for them, and re-layouts  0.8 us (2%)
    pallas_call x1, Pallas kernels, on_device(): pl.pallas_call(kernel, out_shape=jax.ShapeDtypeStruct((TOK, FEAT), BF16),...  42.2 us

profile of v1, /device:TPU:192, one launch (start us, length us, event | category | flops | bytes accessed | tf_op | source)
XLA Modules:
  0.0 43.0 jit_solution(12371194366211906012)
XLA Ops:
  0.0 42.2 %shard_map.37 = bf16[256,1024]{1,0:T(8,128)(2,1)S(1)} custom-call(bf16[256,1024]{1,0:T(8,128)(2,1)} %q_hbm.1, bf16[256,1024]{1,0:T(8,128)(2,1)} %k_hbm.1, bf16[256,1024]{1,0:T(8,128)(2,1)} %v_hbm.1), custom_call_target="tpu_custom_call" | custom-call | tf_op jit(solution)/shard_map/pallas_call | solution.py:403
  42.2 0.8 %copy.5 = bf16[256,1024]{1,0:T(8,128)(2,1)} copy(bf16[256,1024]{1,0:T(8,128)(2,1)S(1)} %shard_map.37) | data formatting | bytes 1048576

commit v2 on v1

--- a/solution.py
+++ b/solution.py
@@ -102,11 +102,13 @@
     near = [(mate, c == 0), (at(x, y, z1, c), zlo == 0), (cross, zlo == 0), (at(x, y1, z, c), y1 > y), (at(x, y2, z, c), y2 > y)]
     near += [(at(xx, y, z, c), xx > x) for xx in [lax.rem(x + d, X) for d in (1, 2, 3)]]
     far_peers = [
-        (at(x, y, zz * 2 + j, c), zz > zhi) for zz in [lax.rem(zhi + d, Z // 2) for d in (3, 2, 1)] for j in range(2)
+        (at(x, y, zz * 2 + j, c), zz > zhi, 4 - d)
+        for d, zz in [(d, lax.rem(zhi + d, Z // 2)) for d in (3, 2, 1)]
+        for j in range(2)
     ]
-    others = [peer for peer, _ in far_peers]
+    others = [peer for peer, _, _ in far_peers]
     end_far = jnp.logical_not(end_near)
-    far_peers += [(end, end_zhi > zhi)]
+    far_peers += [(end, end_zhi > zhi, 0)]
 
     barrier = pltpu.get_barrier_semaphore()
 
@@ -123,15 +125,15 @@
         def _():
             pl.semaphore_wait(sem, amount)
 
-    for peer, later in far_peers + near:
+    for peer, later, *_ in far_peers + near:
         tell(barrier, peer, later)
     await_count(
         barrier,
-        count([jnp.logical_not(later) for _, later in near + far_peers[:-1]]) + (end_zhi < zhi).astype(jnp.int32),
+        count([jnp.logical_not(later) for _, later, *_ in near + far_peers[:-1]]) + (end_zhi < zhi).astype(jnp.int32),
     )
-    for peer, later in far_peers[:-1]:
-        tell(far_sem, peer, jnp.logical_not(later))
-    tell(far_sem, end, end_zhi < zhi)
+    for peer, later, group in far_peers[:-1]:
+        tell(far_sem.at[group], peer, jnp.logical_not(later))
+    tell(far_sem.at[0], end, end_zhi < zhi)
     for peer, later in near:
         tell(near_sem, peer, jnp.logical_not(later))
 
@@ -265,8 +267,11 @@
         arrived(half(xo, 1), first + 3)
 
     def far_sends():
-        await_count(far_sem, count([later for _, later in far_peers]))
-        for copy in far:
+        await_count(far_sem.at[0], (end_zhi > zhi).astype(jnp.int32))
+        await_count(far_sem.at[1], 2 * (zhi == 1).astype(jnp.int32))
+        await_count(far_sem.at[2], 2 * (zhi < 2).astype(jnp.int32))
+        await_count(far_sem.at[3], 2 * (zhi == 0).astype(jnp.int32))
+        for copy in far[:4]:
             copy.start()
         arrived(ybuf.at[pl.ds(0, 2)], 0)
         arrived(ybuf.at[pl.ds(2, 1)], 1)
@@ -291,13 +296,21 @@
 
     send(own.at[:, pl.ds(0, 128)], lvl.at[0], 4, mate)
     send(kv.at[:, rows((1 - c) * LEAF, LEAF)], halo.at[c], 5, mate)
-
-    @pl.when(zhi >= 2)
-    def _():
-        far_sends()
-
     loads[2].wait()
     for_heads(own_tokens)
+
+    await_count(far_sem.at[1], 2 * (lax.rem(zhi, 2) == 0).astype(jnp.int32))
+    for copy in far[4:]:
+        copy.start()
+
+    @pl.when(zhi >= 2)
+    def _():
+        far_sends()
+
+    arrived(lvl.at[0], 4)
+    level(0)
+    arrived(halo.at[1 - c], 5)
+    side(1 - c, 1 - c)
     arrived(lvl.at[1, :, mine], 6)
     send(lvl.at[1, :, mine], lvl.at[1, :, mine], 15, mate)
     passed = jnp.concatenate([average[:32, :64], average[128:144, :64]])
@@ -305,10 +318,8 @@
         derived[i] = jnp.dot(passed, lvl[1, i, mine], preferred_element_type=F32).astype(BF16)
     send(derived.at[:, pl.ds(32, 16)], lvl.at[3, :, rows(c * 64 + 16, 16)], 26, at(x3, y, z, c))
     send(derived.at[:, pl.ds(0, 32)], lvl.at[2, :, rows(c * 64 + 32, 32)], 12, at(x1, y, z, c))
-    arrived(lvl.at[0], 4)
-    level(0)
-    arrived(halo.at[1 - c], 5)
-    side(1 - c, 1 - c)
+    arrived(t5.at[c, x], 8)
+    spread_x(p5, 27)
 
     @pl.when(zhi < 2)
     def _():
@@ -323,22 +334,21 @@
     arrived(lvl.at[3, :, rows(c * 64, 16)], 2)
     arrived(lvl.at[3, :, rows(c * 64 + 16, 16)], 26)
     send(lvl.at[3, :, rows(c * 64, 32)], lvl.at[3, :, rows(c * 64 + 32, 32)], 11, at(x1, y, z, c))
+    relay_x(p5, h5, 27)
     arrived(zbuf.at[pl.ds(0, 7)], 10)
     t8[c, yp, x] = zbuf[:, 2]
     t7[c, x] = zbuf[:, 0:2]
     for d in (1, 2, 3):
         send(p8(x), p8(x), 34 + d, at(lax.rem(x + d, X), y, z, c))
     spread_x(p7, 39)
-    arrived(t5.at[c, x], 8)
-    spread_x(p5, 27)
+
+    @pl.when(passes)
+    def _():
+        arrived(transit, 43)
+        pass_copy.start()
+
     arrived(t6.at[c, x], 9)
     spread_x(p6, 31)
-
-    @pl.when(passes)
-    def _():
-        arrived(transit, 43)
-        pass_copy.start()
-
 
     @pl.when(jnp.logical_not(outer))
     def _():
@@ -347,10 +357,12 @@
     arrived(lvl.at[2, :, rows(c * 64, 32)], 3)
     arrived(lvl.at[2, :, rows(c * 64 + 32, 32)], 12)
     send(lvl.at[2, :, mine], lvl.at[2, :, mine], 14, mate)
+    arrived(lvl.at[2, :, other], 14)
+    level(2)
+    whole_x(h5, 27)
+    send(t5.at[c], t5.at[c], 24, mate)
     arrived(lvl.at[3, :, rows(c * 64 + 32, 32)], 11)
     send(lvl.at[3, :, mine], lvl.at[3, :, mine], 13, mate)
-    arrived(lvl.at[2, :, other], 14)
-    level(2)
     arrived(lvl.at[1, :, other], 15)
     level(1)
     for d in (1, 2, 3):
@@ -358,7 +370,6 @@
     send(t8.at[c, yp], t8.at[c, yp], 20, at(x, y1, z, c))
     send(t8.at[c, yp], t8.at[c, yp], 21, mate)
     relay_x(p7, h7, 39)
-    relay_x(p5, h5, 27)
     relay_x(p6, h6, 31)
     arrived(lvl.at[3, :, other], 13)
     level(3)
@@ -366,17 +377,15 @@
     send(t8.at[c, 1 - yp], t8.at[c, 1 - yp], 25, mate)
     whole_x(h7, 39)
     send(t7.at[c], t7.at[c], 22, mate)
-    whole_x(h5, 27)
-    send(t5.at[c], t5.at[c], 24, mate)
     whole_x(h6, 31)
     send(t6.at[c], t6.at[c], 23, mate)
+    arrived(t5.at[1 - c], 24)
+    deep(t5)
     arrived(t8.at[1 - c, yp], 21)
     arrived(t8.at[1 - c, 1 - yp], 25)
     deep(t8)
     arrived(t7.at[1 - c], 22)
     deep(t7)
-    arrived(t5.at[1 - c], 24)
-    deep(t5)
     arrived(t6.at[1 - c], 23)
     deep(t6)
     arrived(halo.at[c], 7)
@@ -429,7 +438,7 @@
             pltpu.SemaphoreType.DMA((101,)),
             pltpu.SemaphoreType.DMA((44,)),
             pltpu.SemaphoreType.REGULAR,
-            pltpu.SemaphoreType.REGULAR,
+            pltpu.SemaphoreType.REGULAR((4,)),
         ],
         compiler_params=pltpu.CompilerParams(
             collective_id=0, has_side_effects=True, vmem_limit_bytes=24 * 1024 * 1024

time: 43.1 us -> 42.3 us (0.981)
  Pallas kernels: 42.2 us -> 41.4 us
    pallas_call x1, Pallas kernels: 42.2 us -> 41.4 us  [on_device(): pl.pallas_call(kernel, out_shape=jax.ShapeDtypeStruct((TOK, FEAT), BF16),...]
where the time goes in v2:
time: 42.3 us; the launch traced here: 42.2 us
  Pallas kernels  41.4 us (98%)
  local copies, waits for them, and re-layouts  0.8 us (2%)
    pallas_call x1, Pallas kernels, on_device(): pl.pallas_call(kernel, out_shape=jax.ShapeDtypeStruct((TOK, FEAT), BF16),...  41.4 us

profile of v2, /device:TPU:192, one launch (start us, length us, event | category | flops | bytes accessed | tf_op | source)
XLA Modules:
  0.0 42.2 jit_solution(17054149635361698611)
XLA Ops:
  0.0 41.4 %shard_map.37 = bf16[256,1024]{1,0:T(8,128)(2,1)S(1)} custom-call(bf16[256,1024]{1,0:T(8,128)(2,1)} %q_hbm.1, bf16[256,1024]{1,0:T(8,128)(2,1)} %k_hbm.1, bf16[256,1024]{1,0:T(8,128)(2,1)} %v_hbm.1), custom_call_target="tpu_custom_call" | custom-call | tf_op jit(solution)/shard_map/pallas_call | solution.py:412
  41.4 0.8 %copy.5 = bf16[256,1024]{1,0:T(8,128)(2,1)} copy(bf16[256,1024]{1,0:T(8,128)(2,1)S(1)} %shard_map.37) | data formatting | bytes 1048576

commit v3 on v2

--- a/solution.py
+++ b/solution.py
@@ -396,7 +396,7 @@
 
 
     def finish(h, cols):
-        out_ref[:, cols] = (acc[h] / total[h]).T.astype(BF16)
+        out_ref[:, cols] = (acc[h] * (1.0 / total[h])).T.astype(BF16)
 
     for_heads(finish)
 

time: 42.3 us -> 42.3 us (level)
  no operation moved by 1% of the time
where the time goes in v3:
time: 42.3 us; the launch traced here: 42.2 us
  Pallas kernels  41.4 us (98%)
  local copies, waits for them, and re-layouts  0.8 us (2%)
    pallas_call x1, Pallas kernels, on_device(): pl.pallas_call(kernel, out_shape=jax.ShapeDtypeStruct((TOK, FEAT), BF16),...  41.4 us

profile of v3, /device:TPU:192, one launch (start us, length us, event | category | flops | bytes accessed | tf_op | source)
XLA Modules:
  0.0 42.2 jit_solution(8266503703193038994)
XLA Ops:
  0.0 41.4 %shard_map.37 = bf16[256,1024]{1,0:T(8,128)(2,1)S(1)} custom-call(bf16[256,1024]{1,0:T(8,128)(2,1)} %q_hbm.1, bf16[256,1024]{1,0:T(8,128)(2,1)} %k_hbm.1, bf16[256,1024]{1,0:T(8,128)(2,1)} %v_hbm.1), custom_call_target="tpu_custom_call" | custom-call | tf_op jit(solution)/shard_map/pallas_call | solution.py:412
  41.4 0.8 %copy.5 = bf16[256,1024]{1,0:T(8,128)(2,1)} copy(bf16[256,1024]{1,0:T(8,128)(2,1)S(1)} %shard_map.37) | data formatting | bytes 1048576
